TPU v7x, 32 devices: a whole 2x2x4 slice. The times are simulated.
32 devices in a mesh: groups: 2 (over y), ctx: 4 (over z), head: 2 (over x), row: 2 (over core).
Axes of the slice: x: 2, y: 2, z: 4, core: 2. Of those that a mesh axis runs over, the one named last changes fastest.
Arguments:
- residual: bfloat16 [512, 5120], P(('groups', 'ctx', 'row')), parts along dimension 0, may hold values from -6 to 6
- queries: bfloat16 [512, 20, 128], P('groups', 'head'), parts along dimension 0, may hold values from -160 to 160
- incoming_keys: bfloat16 [512, 4, 128], P(('groups', 'ctx', 'row'), 'head'), parts along dimension 0, may hold values from -6 to 6
- incoming_values: bfloat16 [512, 4, 128], P(('groups', 'ctx', 'row'), 'head'), parts along dimension 0, may hold values from -6 to 6
- cache_keys: bfloat16 [32768, 4, 128], P(('groups', 'ctx', 'row'), 'head'), parts along dimension 0, may hold values from -7 to 7
- cached_value_rows: bfloat16 [32768, 4, 128], P(('groups', 'ctx', 'row'), 'head'), parts along dimension 0, may hold values from -6 to 6
- context: int32 [2], P('groups'), parts along dimension 0, may hold values from 4096 to 16384
- attention_out: bfloat16 [2560, 5120], P('head', ('ctx', 'row')), may hold values from -1.5 to 1.5
- mixer_input: bfloat16 [512, 32, 128], P('groups', 'head', ('ctx', 'row')), parts along dimension 0, may hold values from -6 to 6
- mixer_gate: bfloat16 [512, 32, 128], P('groups', 'head', ('ctx', 'row')), parts along dimension 0, may hold values from -6 to 6
- state_in: bfloat16 [512, 256], P('groups'), parts along dimension 0, may hold values from -6 to 6
- state_out: bfloat16 [512, 256], P('groups'), parts along dimension 0, may hold values from -1.5 to 1.5
- step_size: float32 [512, 32], P('groups', 'head'), parts along dimension 0, may hold values from 0 to 2, as said below
- decay_log: float32 [32], P('head'), may hold values from -1 to 1
- skip_gain: float32 [32], P('head'), may hold values from 0.5 to 1.5
- prior_state: float32 [64, 128, 256], P(('groups', 'head'), ('ctx', 'row')), parts along dimension 0, may hold values from -1.5 to 1.5
- mixer_out: bfloat16 [4096, 5120], P('head', ('ctx', 'row')), may hold values from -0.09375 to 0.09375
- norm_gain: float32 [5120], replicated, may hold values from 0.5 to 1.5
- hidden_gate: bfloat16 [5120, 21504], P('head', ('ctx', 'row')), may hold values from -0.078125 to 0.078125
- hidden_up: bfloat16 [5120, 21504], P('head', ('ctx', 'row')), may hold values from -0.078125 to 0.078125
- hidden_down: bfloat16 [21504, 5120], P(('ctx', 'row'), 'head'), may hold values from -0.0390625 to 0.0390625
Outputs:
- block_out: bfloat16 [512, 5120], P(('groups', 'ctx', 'row'), 'head'), parts along dimension 0
There are 2 independent parts, one for each index of `groups`. A program takes and returns all parts, laid end to end along the dimension named above; an argument that names none is the same for every part. Nothing has to cross between parts.
Inputs may be any that keep to these rules, and one draw needn't show every extreme that they name: The cached slots below context are valid; the new tokens follow them. `step_size`: positive.
All inputs are finite; a program needn't handle non-finite values.
Results may differ from a plain program's by a relative error of at most 0.01.
Values may be sent and summed in bfloat16 or wider, within the bound.
A program may use at most 128 MiB of HBM per device.

v0:
```python
import math

import jax
import jax.numpy as jnp
from jax import lax
from jax.sharding import PartitionSpec as P

very_low = -1e30


def combined_all(part, axis, combine):
    gathered = jax.tree.map(lambda a: lax.all_gather(a, axis), part)

    def take(source):
        return jax.tree.map(lambda a: lax.dynamic_index_in_dim(a, source, 0, False), gathered)

    return lax.fori_loop(
        1, lax.axis_size(axis), lambda source, state: combine(state, take(source)), take(0)
    )


def absorb(partial_state, scores, visible, block_values):
    running_sum, weight_total, running_peak = partial_state
    masked = jnp.where(visible, scores, very_low)
    top_score = jnp.maximum(running_peak, jnp.max(masked, axis=3))
    weights = jnp.where(visible, jnp.exp(masked - top_score[..., None]), 0.0)
    fade_factor = jnp.exp(running_peak - top_score)
    mixed_values = jnp.einsum(
        "kgts,skd->kgtd",
        weights.astype(jnp.bfloat16),
        block_values,
        preferred_element_type=jnp.float32,
    )
    return (
        running_sum * fade_factor[..., None] + mixed_values,
        weight_total * fade_factor + jnp.sum(weights, axis=3),
        top_score,
    )


def join_partial(first, second):
    sum_first, total_first, peak_first = first
    sum_second, total_second, peak_second = second
    common = jnp.maximum(peak_first, peak_second)
    fade_first = jnp.exp(peak_first - common)
    fade_second = jnp.exp(peak_second - common)
    return (
        sum_first * fade_first[..., None] + sum_second * fade_second[..., None],
        total_first * fade_first + total_second * fade_second,
        common,
    )


def scan_mixer(
    mixer_input, mixer_gate, state_in, state_out, step_size, decay_log, skip_gain, prior_state
):
    tokens = mixer_input.shape[0]
    decay_rate = -jnp.exp(decay_log)
    log_fade = jnp.cumsum(step_size * decay_rate[None, :], axis=0)
    token_order = jnp.arange(tokens)
    causal_mask = token_order[:, None] >= token_order[None, :]
    fade_heads = jnp.transpose(log_fade)
    differ = fade_heads[:, :, None] - fade_heads[:, None, :]
    lower_fade = jnp.exp(jnp.where(causal_mask[None], differ, very_low))
    state_match = jnp.einsum("tn,sn->ts", state_out, state_in, preferred_element_type=jnp.float32)
    mixing = lower_fade * state_match[None]
    inputs_wide = mixer_input.astype(jnp.float32)
    scaled = step_size[:, :, None] * inputs_wide
    inner_part = jnp.einsum("hts,shp->thp", mixing, scaled, precision=lax.Precision.HIGHEST)
    carried = (
        jnp.einsum(
            "tn,hpn->thp",
            state_out.astype(jnp.float32),
            prior_state,
            precision=lax.Precision.HIGHEST,
        )
        * jnp.exp(log_fade)[:, :, None]
    )
    mixed_out = inner_part + carried + skip_gain[None, :, None] * inputs_wide
    return (mixed_out * jax.nn.silu(mixer_gate.astype(jnp.float32))).astype(jnp.bfloat16)


def on_device(
    residual,
    queries,
    incoming_keys,
    incoming_values,
    cache_keys,
    cached_value_rows,
    context,
    attention_out,
    mixer_input,
    mixer_gate,
    state_in,
    state_out,
    step_size,
    decay_log,
    skip_gain,
    prior_state,
    mixer_out,
    norm_gain,
    hidden_gate,
    hidden_up,
    hidden_down,
):
    tokens = queries.shape[0]
    head_depth = queries.shape[2]
    shared_heads = cache_keys.shape[1]
    group_width = queries.shape[1] // shared_heads
    local_span = cache_keys.shape[0]
    fresh_count = incoming_keys.shape[0]
    owner_index = lax.axis_index(("ctx", "row"))
    score_scale = 1.0 / math.sqrt(head_depth)
    query_view = queries.reshape(tokens, shared_heads, group_width, head_depth)
    block_size = min(512, local_span)
    blocks = local_span // block_size
    key_blocks = cache_keys.reshape(blocks, block_size, shared_heads, head_depth)
    value_blocks = cached_value_rows.reshape(blocks, block_size, shared_heads, head_depth)

    def visit_block(partial_state, inputs):
        block_keys, block_values, block_number = inputs
        scores = (
            jnp.einsum("tkgd,skd->kgts", query_view, block_keys, preferred_element_type=jnp.float32)
            * score_scale
        )
        position = owner_index * local_span + block_number * block_size + jnp.arange(block_size)
        visible = (position < context[0])[None, None, None, :]
        return (absorb(partial_state, scores, visible, block_values), None)

    start_state = (
        jnp.zeros((shared_heads, group_width, tokens, head_depth), jnp.float32),
        jnp.zeros((shared_heads, group_width, tokens), jnp.float32),
        jnp.full((shared_heads, group_width, tokens), very_low, jnp.float32),
    )
    partial_state = lax.scan(
        visit_block, start_state, (key_blocks, value_blocks, jnp.arange(blocks))
    )[0]
    fresh_scores = (
        jnp.einsum("tkgd,skd->kgts", query_view, incoming_keys, preferred_element_type=jnp.float32)
        * score_scale
    )
    source = owner_index * fresh_count + jnp.arange(fresh_count)
    fresh_visible = (source[None, :] <= jnp.arange(tokens)[:, None])[None, None]
    running_sum, weight_total, running_peak = absorb(
        partial_state, fresh_scores, fresh_visible, incoming_values
    )
    merged = combined_all((running_sum, weight_total, running_peak), ("ctx", "row"), join_partial)
    attended = (merged[0] / merged[1][..., None]).astype(jnp.bfloat16)
    attention_part = jnp.einsum(
        "kgtd,kgdc->tc",
        attended,
        attention_out.reshape(shared_heads, group_width, head_depth, -1),
        preferred_element_type=jnp.float32,
    )
    gated = scan_mixer(
        mixer_input, mixer_gate, state_in, state_out, step_size, decay_log, skip_gain, prior_state
    )
    mixer_rows = mixer_out.reshape(mixer_input.shape[1], -1, mixer_out.shape[1])
    mixer_part = jnp.einsum(
        "thp,hpc->tc",
        lax.all_gather(gated, ("ctx", "row"), axis=2, tiled=True),
        mixer_rows,
        preferred_element_type=jnp.float32,
    )
    branches = attention_part + mixer_part
    summed = lax.psum(branches, "head")
    combined = lax.all_to_all(summed, ("ctx", "row"), split_axis=0, concat_axis=1, tiled=True)
    trunk = (residual.astype(jnp.float32) + combined).astype(jnp.bfloat16)
    trunk_wide = trunk.astype(jnp.float32)
    inverse_rms = lax.rsqrt(jnp.mean(trunk_wide * trunk_wide, axis=1, keepdims=True) + 1e-05)
    normed = (trunk_wide * inverse_rms * norm_gain[None, :]).astype(jnp.bfloat16)
    column_count = hidden_gate.shape[0]
    column_start = lax.axis_index("head") * column_count
    normed_part = lax.dynamic_slice_in_dim(normed, column_start, column_count, 1)
    segment = lax.all_gather(normed_part, ("ctx", "row"), axis=0, tiled=True)
    pair_partial = jnp.stack(
        [
            jnp.dot(segment, hidden_gate, preferred_element_type=jnp.float32),
            jnp.dot(segment, hidden_up, preferred_element_type=jnp.float32),
        ]
    )
    pair_share = lax.psum_scatter(pair_partial, "head", scatter_dimension=1, tiled=True)
    hidden_share = (jax.nn.silu(pair_share[0]) * pair_share[1]).astype(jnp.bfloat16)
    hidden = lax.all_gather(hidden_share, "head", axis=0, tiled=True)
    down_rows = lax.psum_scatter(
        jnp.dot(hidden, hidden_down, preferred_element_type=jnp.float32),
        ("ctx", "row"),
        scatter_dimension=0,
        tiled=True,
    )
    trunk_part = lax.dynamic_slice_in_dim(trunk_wide, column_start, column_count, 1)
    return (trunk_part + down_rows).astype(jnp.bfloat16)


def solution(mesh):
    in_specs = (
        P(("groups", "ctx", "row"), None),
        P("groups", "head", None),
        P(("groups", "ctx", "row"), "head", None),
        P(("groups", "ctx", "row"), "head", None),
        P(("groups", "ctx", "row"), "head", None),
        P(("groups", "ctx", "row"), "head", None),
        P("groups"),
        P("head", ("ctx", "row")),
        P("groups", "head", ("ctx", "row")),
        P("groups", "head", ("ctx", "row")),
        P("groups", None),
        P("groups", None),
        P("groups", "head"),
        P("head"),
        P("head"),
        P(("groups", "head"), ("ctx", "row"), None),
        P("head", ("ctx", "row")),
        P(),
        P("head", ("ctx", "row")),
        P("head", ("ctx", "row")),
        P(("ctx", "row"), "head"),
    )
    out_specs = P(("groups", "ctx", "row"), "head")
    return jax.shard_map(
        on_device, mesh=mesh, in_specs=in_specs, out_specs=out_specs, check_vma=False
    )
```

profile of v0, /device:TPU:0, one launch (start us, length us, event | category | flops | bytes accessed | tf_op | source)
XLA Modules:
  0.0 461.1 jit_solution(2985679149651209535)
XLA Ops:
  10.4 5.1 %fusion.43 = f32[256,16,16]{0,2,1:T(8,128)S(1)} fusion(f32[256,256]{1,0:T(8,128)S(1)} %fusion.68, f32[16,256]{1,0:T(8,128)S(1)} %copy_bitcast_fusion.4, pred[256,256]{1,0:T(8,128)(4,1)S(1)} %iota_compare_fusion, bf16[256,16,16]{0,2,1:T(8,128)(2,1)} %param.33, f32[256,16]{0,1:T(8,128)} %param.37), kind=kOutput, calls=%fused_computation.63 | convolution fusion | flops 204603392 | bytes 753664 | tf_op jit(solution)/shard_map/hts,shp->thp/dot_general | solution.py:69
  17.1 67.7 %while.37 = (s32[]{:T(128)}, f32[2,5,256,128]{3,2,1,0:T(8,128)}, f32[2,5,256]{2,1,0:T(8,128)}, f32[2,5,256]{2,1,0:T(8,128)S(1)}, s32[4]{0:T(128)}, /*index=5*/s3...) while((s32[]{:T(128)}, f32[2,5,256,128]{3,2,1,0:T(8,128)}, ...), condition=%wide.region_3.4_spmd.clone, body=%wide.region_0.3_spmd.clone.sunk | while | flops 689124864 | bytes 41802048 | solution.py:135
  17.1 1.3 dynamic_slice.90
  19.7 1.4 constant_dynamic-slice_fusion.3
  21.1 3.8 bitcast_reduce_fusion.2
  25.6 3.7 fusion.94
  29.9 3.1 fusion.96
  33.1 1.3 dynamic_slice.90
  35.6 1.4 constant_dynamic-slice_fusion.3
  37.0 3.8 bitcast_reduce_fusion.2
  41.5 3.7 fusion.94
  45.9 4.5 fusion.96
  52.9 1.4 constant_dynamic-slice_fusion.3
  54.3 3.8 bitcast_reduce_fusion.2
  58.8 3.7 fusion.94
  63.1 4.5 fusion.96
  70.1 1.4 constant_dynamic-slice_fusion.3
  71.5 3.8 bitcast_reduce_fusion.2
  76.0 3.7 fusion.94
  80.3 4.5 fusion.96
  86.8 3.0 convolution_add_fusion
  89.9 15.7 %all-gather.1 = f32[16,5,256]{2,1,0:T(8,128)S(1)} all-gather(f32[2,5,256]{2,1,0:T(8,128)S(1)} %get-tuple-element.400), channel_id=3, replica_groups=mesh['groups'=2,'ctx'=4,'head'=2,'row'=2] {'ctx','row'}, dimensions={0}, use_global_device_ids=true | all-gather | bytes 92160 | tf_op jit(solution)/shard_map/all_gather | solution.py:12
  105.6 16.4 %all-gather.2 = f32[16,5,256]{2,1,0:T(8,128)S(1)} all-gather(f32[2,5,256]{2,1,0:T(8,128)S(1)} %max.18), channel_id=4, replica_groups=mesh['groups'=2,'ctx'=4,'head'=2,'row'=2] {'ctx','row'}, dimensions={0}, use_global_device_ids=true | all-gather | bytes 92160 | tf_op jit(solution)/shard_map/all_gather | solution.py:12
  122.0 3.1 convolution_bitcast_fusion.2
  125.1 68.0 %all-gather.14.cloned.1.call-done = f32[16,5,256,128]{3,2,1,0:T(8,128)} async-done(((f32[2,5,256,128]{3,2,1,0:T(8,128)}), f32[16,5,256,128]{3,2,1,0:T(8,128)}) %all-gather.14.cloned.1.call-update) | async-done | bytes 10485776 | tf_op jit(solution)/shard_map/all_gather | solution.py:12
  193.1 1.4 slice.22
  194.5 14.7 %while.36 = (s32[]{:T(128)}, f32[2,5,256,128]{3,2,1,0:T(8,128)S(1)}, f32[2,5,256]{2,1,0:T(8,128)S(1)}, f32[2,5,256]{2,1,0:T(8,128)S(1)}, f32[8,2,5,256]{3,2,1,0:...) while((s32[]{:T(128)}, ...), condition=%wide.region_7.8_spmd, body=%wide.region_6.7_spmd.sunk | while | flops 998405 | bytes 4034711 | solution.py:17
  194.6 2.1 fusion.91
  196.7 2.0 fusion.91
  198.8 2.0 fusion.91
  200.9 2.0 fusion.91
  203.0 2.0 fusion.91
  205.1 2.0 fusion.91
  207.2 2.0 fusion.91
  209.2 3.0 fusion.36
  212.3 30.0 %all-reduce.2.cloned.1.call-done = f32[8,32,640]{2,1,0:T(8,128)} async-done(((f32[8,32,640]{2,1,0:T(8,128)}), f32[8,32,640]{2,1,0:T(8,128)}) %all-reduce.2.cloned.1.call-update) | async-done | bytes 655376 | tf_op jit(solution)/shard_map/psum | solution.py:166
  242.3 4.6 all-to-all-start
  247.0 18.0 %all-to-all-done = f32[8,32,640]{2,1,0:T(8,128)S(1)} async-done(((f32[8,32,640]{2,1,0:T(8,128)}), f32[8,32,640]{2,1,0:T(8,128)S(1)}, u32[]{:S(2)}, u32[]{:S(2)}) %all-to-all-start) | async-done | bytes 655392 | tf_op jit(solution)/shard_map/all_to_all | solution.py:167
  266.2 21.5 %all-gather.10.cloned.1.call-done = bf16[256,2560]{1,0:T(8,128)(2,1)} async-done(((bf16[32,2560]{1,0:T(8,128)(2,1)}), bf16[256,2560]{1,0:T(8,128)(2,1)}) %all-gather.10.cloned.1.call-update) | async-done | bytes 1310736 | tf_op jit(solution)/shard_map/all_gather | solution.py:175
  287.7 9.7 %convolution_bitcast_fusion = f32[1,256,2688]{2,1,0:T(8,128)S(1)} fusion(bf16[256,2560]{1,0:T(8,128)(2,1)} %all-gather.10.cloned.1.call-done, bf16[2560,2688]{1,0:T(8,128)(2,1)} %param.44), kind=kOutput, calls=%fused_computation.39 | convolution fusion | flops 3523215360 | bytes 17825792 | tf_op jit(solution)/shard_map/dot_general | solution.py:179
  297.4 7.5 %convolution_bitcast_fusion.1 = f32[1,256,2688]{2,1,0:T(8,128)S(1)} fusion(bf16[256,2560]{1,0:T(8,128)(2,1)S(1)} %copy-done.11, bf16[2560,2688]{1,0:T(8,128)(2,1)} %param.43), kind=kOutput, calls=%fused_computation.40 | convolution fusion | flops 3523215360 | bytes 17825792 | tf_op jit(solution)/shard_map/dot_general | solution.py:178
  304.9 2.8 pad_maximum_fusion
  307.7 68.1 %reduce-scatter.3.cloned.1.call-done = f32[2,128,2688]{2,1,0:T(8,128)} async-done(((f32[2,256,2688]{2,1,0:T(8,128)}), f32[2,128,2688]{2,1,0:T(8,128)}) %reduce-scatter.3.cloned.1.call-update) | async-done | bytes 2752528 | tf_op jit(solution)/shard_map/reduce_scatter | solution.py:182
  375.8 3.0 fusion.32
  378.9 25.1 %all-gather.12.cloned.1.call-done = bf16[256,2688]{1,0:T(8,128)(2,1)} async-done(((bf16[128,2688]{1,0:T(8,128)(2,1)}), bf16[256,2688]{1,0:T(8,128)(2,1)}) %all-gather.12.cloned.1.call-update) | async-done | bytes 1376272 | tf_op jit(solution)/shard_map/all_gather | solution.py:184
  404.0 10.8 %fusion.69 = f32[256,2560]{1,0:T(8,128)} fusion(bf16[256,2688]{1,0:T(8,128)(2,1)} %all-gather.12.cloned.1.call-done, bf16[2688,2560]{1,0:T(8,128)(2,1)} %param.45), kind=kOutput, calls=%fused_computation.106 | convolution fusion | flops 3523215360 | bytes 17760256 | tf_op jit(solution)/shard_map/dot_general | solution.py:186
  414.9 37.7 %reduce-scatter.5.cloned.1.call-done = f32[32,2560]{1,0:T(8,128)} async-done(((f32[256,2560]{1,0:T(8,128)}), f32[32,2560]{1,0:T(8,128)}) %reduce-scatter.5.cloned.1.call-update) | async-done | bytes 327696 | tf_op jit(solution)/shard_map/reduce_scatter | solution.py:185
  452.6 1.7 add_convert_fusion.1
  (132 shorter events, 19.5 us)
Async XLA Ops:
  6.5 115.4 %copy-start = (bf16[2048,640]{1,0:T(8,128)(2,1)S(1)}, bf16[2048,640]{1,0:T(8,128)(2,1)}, u32[]{:S(2)}) copy-start(bf16[2048,640]{1,0:T(8,128)(2,1)} %param.41) | copy-start | bytes 7864324
  6.5 115.4 %all-gather.8.cloned.1.call-start = ((), (), s32[]{:S(2)}) async-start(), calls=%async_computation.3 | async-start | bytes 1179648 | tf_op jit(solution)/shard_map/all_gather | solution.py:161
  10.3 5.1 %copy-start.9 = (bf16[256,256]{1,0:T(8,128)(2,1)S(1)}, bf16[256,256]{1,0:T(8,128)(2,1)}, u32[]{:S(2)}) copy-start(bf16[256,256]{1,0:T(8,128)(2,1)} %param.36) | copy-start | bytes 393220
  10.3 5.1 %copy-start.12 = (f32[16,16,256]{2,1,0:T(8,128)S(1)}, f32[16,16,256]{2,1,0:T(8,128)}, u32[]{:S(2)}) copy-start(f32[16,16,256]{2,1,0:T(8,128)} %param.40) | copy-start | bytes 786436
  10.3 5.1 %copy-start.13 = (bf16[256,16,16]{0,2,1:T(8,128)(2,1)S(1)}, bf16[256,16,16]{0,2,1:T(8,128)(2,1)}, u32[]{:S(2)}) copy-start(bf16[256,16,16]{0,2,1:T(8,128)(2,1)} %param.33) | copy-start | bytes 393220
  10.3 5.1 %copy-start.14 = (bf16[256,16,16]{0,2,1:T(8,128)(2,1)S(1)}, bf16[256,16,16]{0,2,1:T(8,128)(2,1)}, u32[]{:S(2)}) copy-start(bf16[256,16,16]{0,2,1:T(8,128)(2,1)} %param.34) | copy-start | bytes 393220
  10.3 5.1 %copy-start.15 = (f32[16]{0:T(128)S(1)}, f32[16]{0:T(128)}, u32[]{:S(2)}) copy-start(f32[16]{0:T(128)} %param.39) | copy-start | bytes 196
  10.4 6.8 %copy-start.3 = (bf16[256,10,128]{2,0,1:T(8,128)(2,1)S(1)}, bf16[256,10,128]{2,0,1:T(8,128)(2,1)}, u32[]{:S(2)}) copy-start(bf16[256,10,128]{2,0,1:T(8,128)(2,1)} %param.26) | copy-start | bytes 1966084
  16.5 176.6 %all-gather.14.cloned.1.call-start = ((), (), s32[]{:S(2)}) async-start(), calls=%async_computation.9 | async-start | bytes 11796480 | tf_op jit(solution)/shard_map/all_gather | solution.py:12
  19.7 5.2 %copy-start.7 = (pred[512]{0:T(512)(128)(4,1)}, pred[512]{0:T(512)(128)(4,1)S(1)}, u32[]{:S(2)}) copy-start(pred[512]{0:T(512)(128)(4,1)S(1)} %add_compare_fusion.2) | copy-start | bytes 1540 | tf_op jit(solution)/shard_map/while
  25.6 3.7 copy-start.4
  25.6 4.3 copy-start.2
  25.6 4.3 copy-start.8
  29.3 0.6 copy-start.5
  35.6 5.2 %copy-start.7 = (pred[512]{0:T(512)(128)(4,1)}, pred[512]{0:T(512)(128)(4,1)S(1)}, u32[]{:S(2)}) copy-start(pred[512]{0:T(512)(128)(4,1)S(1)} %add_compare_fusion.2) | copy-start | bytes 1540 | tf_op jit(solution)/shard_map/while
  41.5 3.7 copy-start.4
  41.5 4.3 copy-start.2
  41.5 4.3 copy-start.8
  45.3 0.6 copy-start.5
  52.9 5.2 %copy-start.7 = (pred[512]{0:T(512)(128)(4,1)}, pred[512]{0:T(512)(128)(4,1)S(1)}, u32[]{:S(2)}) copy-start(pred[512]{0:T(512)(128)(4,1)S(1)} %add_compare_fusion.2) | copy-start | bytes 1540 | tf_op jit(solution)/shard_map/while
  58.8 3.7 copy-start.4
  58.8 4.3 copy-start.2
  58.8 4.3 copy-start.8
  62.5 0.6 copy-start.5
  70.1 5.2 %copy-start.7 = (pred[512]{0:T(512)(128)(4,1)}, pred[512]{0:T(512)(128)(4,1)S(1)}, u32[]{:S(2)}) copy-start(pred[512]{0:T(512)(128)(4,1)S(1)} %add_compare_fusion.2) | copy-start | bytes 1540 | tf_op jit(solution)/shard_map/while
  76.0 3.7 copy-start.4
  76.0 4.3 copy-start.2
  76.0 4.3 copy-start.8
  79.7 0.6 copy-start.5
  89.8 152.5 %all-reduce.2.cloned.1.call-start = ((), (), s32[]{:S(2)}) async-start(), calls=%async_computation.4 | async-start | bytes 1310720 | tf_op jit(solution)/shard_map/psum | solution.py:166
  194.5 14.7 %copy-start.16 = (f32[256,640]{1,0:T(8,128)S(1)}, f32[256,640]{1,0:T(8,128)}, u32[]{:S(2)}) copy-start(f32[256,640]{1,0:T(8,128)} %convolution_bitcast_fusion.2) | copy-start | bytes 1966084
  209.2 37.7 %copy-start.10 = (f32[5120]{0:T(1024)S(1)}, f32[5120]{0:T(1024)}, u32[]{:S(2)}) copy-start(f32[5120]{0:T(1024)} %param.42) | copy-start | bytes 61444
  212.3 52.8 %copy-start.6 = (bf16[32,5120]{1,0:T(8,128)(2,1)S(1)}, bf16[32,5120]{1,0:T(8,128)(2,1)}, u32[]{:S(2)}) copy-start(bf16[32,5120]{1,0:T(8,128)(2,1)} %param.25) | copy-start | bytes 983044
  242.3 22.8 %all-to-all-start = ((f32[8,32,640]{2,1,0:T(8,128)}), f32[8,32,640]{2,1,0:T(8,128)S(1)}, u32[]{:S(2)}, u32[]{:S(2)}) async-start(f32[8,32,640]{2,1,0:T(8,128)} %all-reduce.2.cloned.1.call-done), calls=%async_computation | async-start | bytes 1310720 | tf_op jit(solution)/shard_map/all_to_all | solution.py:167
  246.9 40.8 %all-gather.10.cloned.1.call-start = ((), (), s32[]{:S(2)}) async-start(), calls=%async_computation.5 | async-start | bytes 1474560 | tf_op jit(solution)/shard_map/all_gather | solution.py:175
  266.1 109.7 %reduce-scatter.3.cloned.1.call-start = ((), (), s32[]{:S(2)}) async-start(), calls=%async_computation.6 | async-start | bytes 8257536 | tf_op jit(solution)/shard_map/reduce_scatter | solution.py:182
  287.7 9.7 %copy-start.11 = (bf16[256,2560]{1,0:T(8,128)(2,1)S(1)}, bf16[256,2560]{1,0:T(8,128)(2,1)}, u32[]{:S(2)}) copy-start(bf16[256,2560]{1,0:T(8,128)(2,1)} %all-gather.10.cloned.1.call-done) | copy-start | bytes 3932164
  307.7 96.3 %all-gather.12.cloned.1.call-start = ((), (), s32[]{:S(2)}) async-start(), calls=%async_computation.7 | async-start | bytes 2064384 | tf_op jit(solution)/shard_map/all_gather | solution.py:184
  378.8 73.7 %reduce-scatter.5.cloned.1.call-start = ((), (), s32[]{:S(2)}) async-start(), calls=%async_computation.8 | async-start | bytes 2949120 | tf_op jit(solution)/shard_map/reduce_scatter | solution.py:185
  404.0 50.2 %copy-start.1 = (bf16[2048,640]{1,0:T(8,128)(2,1)S(1)}, bf16[2048,640]{1,0:T(8,128)(2,1)}, u32[]{:S(2)}) copy-start(bf16[2048,640]{1,0:T(8,128)(2,1)} %param.41) | copy-start | bytes 7864324
Sparse Core Ops, SparseCore 0:
  16.6 24.7 all-gather.7
  89.9 103.1 all-gather.13
  212.4 29.8 all-reduce.1
  266.3 21.3 all-gather.9
  307.8 67.9 reduce-scatter.2
  379.0 24.9 all-gather.11
  415.0 37.5 reduce-scatter.4
where the time goes:
time: 462 us; the launch traced here: 461 us
  waiting for transfers between devices  269 us (58%)
  matrix products  77.1 us (17%)
  other arithmetic  46.4 us (10%)
  blocking collectives  32.1 us (7%)
  local copies, waits for them, and re-layouts  15.3 us (3%)
  between operations  13.8 us (3%)
  starting transfers between devices  4.85 us (1%)
    reduce_scatter x1, waiting for transfers between devices, on_device(): lax.psum_scatter(pair_partial, 'head', scatter_dimension=1, tiled=True)  68.1 us
    all_gather x1, waiting for transfers between devices, combined_all(): gathered = jax.tree.map(lambda a: lax.all_gather(a, axis), part)  68 us
    reduce_scatter x1, waiting for transfers between devices, on_device(): lax.psum_scatter(jnp.dot(hidden, hidden_down, preferred_element_type=jnp....  37.7 us
    all_gather x2, blocking collectives, combined_all(): gathered = jax.tree.map(lambda a: lax.all_gather(a, axis), part)  32.1 us
    psum x1, waiting for transfers between devices, on_device(): summed = lax.psum(branches, 'head')  30 us
    all_gather x1, waiting for transfers between devices, on_device(): hidden = lax.all_gather(hidden_share, 'head', axis=0, tiled=True)  25.1 us
    all_gather x1, waiting for transfers between devices, on_device(): segment = lax.all_gather(normed_part, ('ctx', 'row'), axis=0, tiled=True)  21.5 us
    dot_general x5, matrix products, absorb(): jnp.einsum('kgts,skd->kgtd', weights.astype(jnp.bfloat16), block_values,...  19.5 us
  transfers between devices with their start and end apart: 8, of which 7 were waited for; matrix products, arithmetic and copies ran while one was open for 15% of the time, Pallas kernels for 0%

commit v1 on v0

--- a/solution.py
+++ b/solution.py
@@ -56,9 +56,13 @@
 ):
     tokens = mixer_input.shape[0]
     decay_rate = -jnp.exp(decay_log)
-    log_fade = jnp.cumsum(step_size * decay_rate[None, :], axis=0)
     token_order = jnp.arange(tokens)
     causal_mask = token_order[:, None] >= token_order[None, :]
+    log_fade = jnp.dot(
+        causal_mask.astype(jnp.float32),
+        step_size * decay_rate[None, :],
+        precision=lax.Precision.HIGHEST,
+    )
     fade_heads = jnp.transpose(log_fade)
     differ = fade_heads[:, :, None] - fade_heads[:, None, :]
     lower_fade = jnp.exp(jnp.where(causal_mask[None], differ, very_low))

time: 462 us -> 462 us (level)
  transfers between devices with their start and end apart: 8 -> 8, of which waited for: 7 -> 7; matrix products, arithmetic and copies ran while one was open for 15% -> 16% of each run, Pallas kernels for 0% -> 0%
where the time goes in v1:
time: 462 us; the launch traced here: 460 us
  waiting for transfers between devices  268 us (58%)
  matrix products  78.1 us (17%)
  other arithmetic  45.4 us (10%)
  blocking collectives  32.1 us (7%)
  local copies, waits for them, and re-layouts  14.9 us (3%)
  between operations  13.8 us (3%)
  starting transfers between devices  4.85 us (1%)
    reduce_scatter x1, waiting for transfers between devices, on_device(): lax.psum_scatter(pair_partial, 'head', scatter_dimension=1, tiled=True)  68.1 us
    all_gather x1, waiting for transfers between devices, combined_all(): gathered = jax.tree.map(lambda a: lax.all_gather(a, axis), part)  68 us
    reduce_scatter x1, waiting for transfers between devices, on_device(): lax.psum_scatter(jnp.dot(hidden, hidden_down, preferred_element_type=jnp....  37.7 us
    all_gather x2, blocking collectives, combined_all(): gathered = jax.tree.map(lambda a: lax.all_gather(a, axis), part)  32.1 us
    psum x1, waiting for transfers between devices, on_device(): summed = lax.psum(branches, 'head')  30 us
    all_gather x1, waiting for transfers between devices, on_device(): hidden = lax.all_gather(hidden_share, 'head', axis=0, tiled=True)  25.1 us
    all_gather x1, waiting for transfers between devices, on_device(): segment = lax.all_gather(normed_part, ('ctx', 'row'), axis=0, tiled=True)  21.5 us
    dot_general x5, matrix products, absorb(): jnp.einsum('kgts,skd->kgtd', weights.astype(jnp.bfloat16), block_values,...  19.4 us
  transfers between devices with their start and end apart: 8, of which 7 were waited for; matrix products, arithmetic and copies ran while one was open for 16% of the time, Pallas kernels for 0%

profile of v1, /device:TPU:0, one launch (start us, length us, event | category | flops | bytes accessed | tf_op | source)
XLA Modules:
  0.0 460.3 jit_solution(16193421208455415371)
XLA Ops:
  8.4 1.2 fusion.72
  9.6 5.1 %fusion.43 = f32[256,16,16]{0,2,1:T(8,128)S(1)} fusion(f32[256,256]{1,0:T(8,128)S(1)} %fusion.72, f32[16,256]{1,0:T(8,128)S(1)} %bitcast.137, pred[256,256]{1,0:T(8,128)(4,1)S(1)} %iota_compare_fusion, bf16[256,16,16]{0,2,1:T(8,128)(2,1)} %param.33, f32[256,16]{0,1:T(8,128)} %param.37), kind=kOutput, calls=%fused_computation.63 | convolution fusion | flops 204603392 | bytes 753664 | tf_op jit(solution)/shard_map/hts,shp->thp/dot_general | solution.py:73
  16.4 67.7 %while.37 = (s32[]{:T(128)}, f32[2,5,256,128]{3,2,1,0:T(8,128)}, f32[2,5,256]{2,1,0:T(8,128)}, f32[2,5,256]{2,1,0:T(8,128)S(1)}, s32[4]{0:T(128)}, /*index=5*/s3...) while((s32[]{:T(128)}, f32[2,5,256,128]{3,2,1,0:T(8,128)}, ...), condition=%wide.region_3.4_spmd.clone, body=%wide.region_0.3_spmd.clone.sunk | while | flops 689124864 | bytes 41802048 | solution.py:139
  16.4 1.2 dynamic_slice.90
  18.8 1.4 constant_dynamic-slice_fusion.3
  20.2 3.8 bitcast_reduce_fusion.2
  24.8 3.8 fusion.98
  29.2 3.1 fusion.100
  34.7 1.4 constant_dynamic-slice_fusion.3
  36.2 3.8 bitcast_reduce_fusion.2
  40.7 3.8 fusion.98
  45.2 4.4 fusion.100
  52.0 1.4 constant_dynamic-slice_fusion.3
  53.4 3.8 bitcast_reduce_fusion.2
  58.0 3.8 fusion.98
  62.4 4.4 fusion.100
  69.3 1.4 constant_dynamic-slice_fusion.3
  70.7 3.8 bitcast_reduce_fusion.2
  75.2 3.8 fusion.98
  79.7 4.4 fusion.100
  86.1 3.0 convolution_add_fusion
  89.2 15.7 %all-gather.1 = f32[16,5,256]{2,1,0:T(8,128)S(1)} all-gather(f32[2,5,256]{2,1,0:T(8,128)S(1)} %get-tuple-element.400), channel_id=3, replica_groups=mesh['groups'=2,'ctx'=4,'head'=2,'row'=2] {'ctx','row'}, dimensions={0}, use_global_device_ids=true | all-gather | bytes 92160 | tf_op jit(solution)/shard_map/all_gather | solution.py:12
  104.9 16.4 %all-gather.2 = f32[16,5,256]{2,1,0:T(8,128)S(1)} all-gather(f32[2,5,256]{2,1,0:T(8,128)S(1)} %max.18), channel_id=4, replica_groups=mesh['groups'=2,'ctx'=4,'head'=2,'row'=2] {'ctx','row'}, dimensions={0}, use_global_device_ids=true | all-gather | bytes 92160 | tf_op jit(solution)/shard_map/all_gather | solution.py:12
  121.3 3.1 convolution_bitcast_fusion.2
  124.4 68.0 %all-gather.14.cloned.1.call-done = f32[16,5,256,128]{3,2,1,0:T(8,128)} async-done(((f32[2,5,256,128]{3,2,1,0:T(8,128)}), f32[16,5,256,128]{3,2,1,0:T(8,128)}) %all-gather.14.cloned.1.call-update) | async-done | bytes 10485776 | tf_op jit(solution)/shard_map/all_gather | solution.py:12
  192.4 1.4 slice.14
  193.8 14.7 %while.36 = (s32[]{:T(128)}, f32[2,5,256,128]{3,2,1,0:T(8,128)S(1)}, f32[2,5,256]{2,1,0:T(8,128)S(1)}, f32[2,5,256]{2,1,0:T(8,128)S(1)}, f32[8,2,5,256]{3,2,1,0:...) while((s32[]{:T(128)}, ...), condition=%wide.region_7.8_spmd, body=%wide.region_6.7_spmd.sunk | while | flops 998405 | bytes 4034711 | solution.py:17
  193.8 2.1 fusion.95
  196.0 2.0 fusion.95
  198.1 2.0 fusion.95
  200.2 2.0 fusion.95
  202.3 2.0 fusion.95
  204.4 2.0 fusion.95
  206.4 2.0 fusion.95
  208.5 3.1 fusion.36
  211.6 30.0 %all-reduce.2.cloned.1.call-done = f32[8,32,640]{2,1,0:T(8,128)} async-done(((f32[8,32,640]{2,1,0:T(8,128)}), f32[8,32,640]{2,1,0:T(8,128)}) %all-reduce.2.cloned.1.call-update) | async-done | bytes 655376 | tf_op jit(solution)/shard_map/psum | solution.py:170
  241.6 4.6 %all-to-all-start = ((f32[8,32,640]{2,1,0:T(8,128)}), f32[8,32,640]{2,1,0:T(8,128)S(1)}, u32[]{:S(2)}, u32[]{:S(2)}) async-start(f32[8,32,640]{2,1,0:T(8,128)} %all-reduce.2.cloned.1.call-done), calls=%async_computation | async-start | bytes 1310720 | tf_op jit(solution)/shard_map/all_to_all | solution.py:171
  246.3 18.0 %all-to-all-done = f32[8,32,640]{2,1,0:T(8,128)S(1)} async-done(((f32[8,32,640]{2,1,0:T(8,128)}), f32[8,32,640]{2,1,0:T(8,128)S(1)}, u32[]{:S(2)}, u32[]{:S(2)}) %all-to-all-start) | async-done | bytes 655392 | tf_op jit(solution)/shard_map/all_to_all | solution.py:171
  265.5 21.5 %all-gather.10.cloned.1.call-done = bf16[256,2560]{1,0:T(8,128)(2,1)} async-done(((bf16[32,2560]{1,0:T(8,128)(2,1)}), bf16[256,2560]{1,0:T(8,128)(2,1)}) %all-gather.10.cloned.1.call-update) | async-done | bytes 1310736 | tf_op jit(solution)/shard_map/all_gather | solution.py:179
  287.0 9.7 %convolution_bitcast_fusion = f32[1,256,2688]{2,1,0:T(8,128)S(1)} fusion(bf16[256,2560]{1,0:T(8,128)(2,1)} %all-gather.10.cloned.1.call-done, bf16[2560,2688]{1,0:T(8,128)(2,1)} %param.44), kind=kOutput, calls=%fused_computation.39 | convolution fusion | flops 3523215360 | bytes 17825792 | tf_op jit(solution)/shard_map/dot_general | solution.py:183
  296.6 7.5 %convolution_bitcast_fusion.1 = f32[1,256,2688]{2,1,0:T(8,128)S(1)} fusion(bf16[256,2560]{1,0:T(8,128)(2,1)S(1)} %copy-done.11, bf16[2560,2688]{1,0:T(8,128)(2,1)} %param.43), kind=kOutput, calls=%fused_computation.40 | convolution fusion | flops 3523215360 | bytes 17825792 | tf_op jit(solution)/shard_map/dot_general | solution.py:182
  304.2 2.8 pad_maximum_fusion
  307.0 68.1 %reduce-scatter.3.cloned.1.call-done = f32[2,128,2688]{2,1,0:T(8,128)} async-done(((f32[2,256,2688]{2,1,0:T(8,128)}), f32[2,128,2688]{2,1,0:T(8,128)}) %reduce-scatter.3.cloned.1.call-update) | async-done | bytes 2752528 | tf_op jit(solution)/shard_map/reduce_scatter | solution.py:186
  375.1 3.0 fusion.32
  378.2 25.1 %all-gather.12.cloned.1.call-done = bf16[256,2688]{1,0:T(8,128)(2,1)} async-done(((bf16[128,2688]{1,0:T(8,128)(2,1)}), bf16[256,2688]{1,0:T(8,128)(2,1)}) %all-gather.12.cloned.1.call-update) | async-done | bytes 1376272 | tf_op jit(solution)/shard_map/all_gather | solution.py:188
  403.3 10.9 %fusion.73 = f32[256,2560]{1,0:T(8,128)} fusion(bf16[256,2688]{1,0:T(8,128)(2,1)} %all-gather.12.cloned.1.call-done, bf16[2688,2560]{1,0:T(8,128)(2,1)} %param.45), kind=kOutput, calls=%fused_computation.104 | convolution fusion | flops 3523215360 | bytes 17760256 | tf_op jit(solution)/shard_map/dot_general | solution.py:190
  414.1 37.7 %reduce-scatter.5.cloned.1.call-done = f32[32,2560]{1,0:T(8,128)} async-done(((f32[256,2560]{1,0:T(8,128)}), f32[32,2560]{1,0:T(8,128)}) %reduce-scatter.5.cloned.1.call-update) | async-done | bytes 327696 | tf_op jit(solution)/shard_map/reduce_scatter | solution.py:189
  451.8 1.7 add_convert_fusion.1
  (126 shorter events, 18.6 us)
Async XLA Ops:
  6.5 114.8 %copy-start = (bf16[2048,640]{1,0:T(8,128)(2,1)S(1)}, bf16[2048,640]{1,0:T(8,128)(2,1)}, u32[]{:S(2)}) copy-start(bf16[2048,640]{1,0:T(8,128)(2,1)} %param.41) | copy-start | bytes 7864324
  6.5 114.8 %all-gather.8.cloned.1.call-start = ((), (), s32[]{:S(2)}) async-start(), calls=%async_computation.3 | async-start | bytes 1179648 | tf_op jit(solution)/shard_map/all_gather | solution.py:165
  9.6 5.1 %copy-start.9 = (bf16[256,256]{1,0:T(8,128)(2,1)S(1)}, bf16[256,256]{1,0:T(8,128)(2,1)}, u32[]{:S(2)}) copy-start(bf16[256,256]{1,0:T(8,128)(2,1)} %param.36) | copy-start | bytes 393220
  9.6 5.1 %copy-start.12 = (f32[16,16,256]{2,1,0:T(8,128)S(1)}, f32[16,16,256]{2,1,0:T(8,128)}, u32[]{:S(2)}) copy-start(f32[16,16,256]{2,1,0:T(8,128)} %param.40) | copy-start | bytes 786436
  9.6 5.1 %copy-start.13 = (bf16[256,16,16]{0,2,1:T(8,128)(2,1)S(1)}, bf16[256,16,16]{0,2,1:T(8,128)(2,1)}, u32[]{:S(2)}) copy-start(bf16[256,16,16]{0,2,1:T(8,128)(2,1)} %param.33) | copy-start | bytes 393220
  9.6 5.1 %copy-start.14 = (bf16[256,16,16]{0,2,1:T(8,128)(2,1)S(1)}, bf16[256,16,16]{0,2,1:T(8,128)(2,1)}, u32[]{:S(2)}) copy-start(bf16[256,16,16]{0,2,1:T(8,128)(2,1)} %param.34) | copy-start | bytes 393220
  9.6 5.1 %copy-start.15 = (f32[16]{0:T(128)S(1)}, f32[16]{0:T(128)}, u32[]{:S(2)}) copy-start(f32[16]{0:T(128)} %param.39) | copy-start | bytes 196
  9.6 6.8 %copy-start.3 = (bf16[256,10,128]{2,0,1:T(8,128)(2,1)S(1)}, bf16[256,10,128]{2,0,1:T(8,128)(2,1)}, u32[]{:S(2)}) copy-start(bf16[256,10,128]{2,0,1:T(8,128)(2,1)} %param.26) | copy-start | bytes 1966084
  15.8 176.6 %all-gather.14.cloned.1.call-start = ((), (), s32[]{:S(2)}) async-start(), calls=%async_computation.9 | async-start | bytes 11796480 | tf_op jit(solution)/shard_map/all_gather | solution.py:12
  18.8 5.2 %copy-start.7 = (pred[512]{0:T(512)(128)(4,1)}, pred[512]{0:T(512)(128)(4,1)S(1)}, u32[]{:S(2)}) copy-start(pred[512]{0:T(512)(128)(4,1)S(1)} %add_compare_fusion.2) | copy-start | bytes 1540 | tf_op jit(solution)/shard_map/while
  24.8 3.8 copy-start.4
  24.8 4.5 copy-start.2
  24.8 4.5 copy-start.8
  28.6 0.6 copy-start.5
  34.7 5.3 %copy-start.7 = (pred[512]{0:T(512)(128)(4,1)}, pred[512]{0:T(512)(128)(4,1)S(1)}, u32[]{:S(2)}) copy-start(pred[512]{0:T(512)(128)(4,1)S(1)} %add_compare_fusion.2) | copy-start | bytes 1540 | tf_op jit(solution)/shard_map/while
  40.7 3.8 copy-start.4
  40.7 4.5 copy-start.2
  40.7 4.5 copy-start.8
  44.6 0.6 copy-start.5
  52.0 5.2 %copy-start.7 = (pred[512]{0:T(512)(128)(4,1)}, pred[512]{0:T(512)(128)(4,1)S(1)}, u32[]{:S(2)}) copy-start(pred[512]{0:T(512)(128)(4,1)S(1)} %add_compare_fusion.2) | copy-start | bytes 1540 | tf_op jit(solution)/shard_map/while
  58.0 3.8 copy-start.4
  58.0 4.5 copy-start.2
  58.0 4.5 copy-start.8
  61.8 0.6 copy-start.5
  69.2 5.2 %copy-start.7 = (pred[512]{0:T(512)(128)(4,1)}, pred[512]{0:T(512)(128)(4,1)S(1)}, u32[]{:S(2)}) copy-start(pred[512]{0:T(512)(128)(4,1)S(1)} %add_compare_fusion.2) | copy-start | bytes 1540 | tf_op jit(solution)/shard_map/while
  75.2 3.8 copy-start.4
  75.2 4.5 copy-start.2
  75.2 4.5 copy-start.8
  79.1 0.6 copy-start.5
  89.1 152.5 %all-reduce.2.cloned.1.call-start = ((), (), s32[]{:S(2)}) async-start(), calls=%async_computation.4 | async-start | bytes 1310720 | tf_op jit(solution)/shard_map/psum | solution.py:170
  193.8 14.7 %copy-start.16 = (f32[256,640]{1,0:T(8,128)S(1)}, f32[256,640]{1,0:T(8,128)}, u32[]{:S(2)}) copy-start(f32[256,640]{1,0:T(8,128)} %convolution_bitcast_fusion.2) | copy-start | bytes 1966084
  208.5 37.7 %copy-start.10 = (f32[5120]{0:T(1024)S(1)}, f32[5120]{0:T(1024)}, u32[]{:S(2)}) copy-start(f32[5120]{0:T(1024)} %param.42) | copy-start | bytes 61444
  211.6 52.8 %copy-start.6 = (bf16[32,5120]{1,0:T(8,128)(2,1)S(1)}, bf16[32,5120]{1,0:T(8,128)(2,1)}, u32[]{:S(2)}) copy-start(bf16[32,5120]{1,0:T(8,128)(2,1)} %param.25) | copy-start | bytes 983044
  241.6 22.8 %all-to-all-start = ((f32[8,32,640]{2,1,0:T(8,128)}), f32[8,32,640]{2,1,0:T(8,128)S(1)}, u32[]{:S(2)}, u32[]{:S(2)}) async-start(f32[8,32,640]{2,1,0:T(8,128)} %all-reduce.2.cloned.1.call-done), calls=%async_computation | async-start | bytes 1310720 | tf_op jit(solution)/shard_map/all_to_all | solution.py:171
  246.2 40.8 %all-gather.10.cloned.1.call-start = ((), (), s32[]{:S(2)}) async-start(), calls=%async_computation.5 | async-start | bytes 1474560 | tf_op jit(solution)/shard_map/all_gather | solution.py:179
  265.4 109.7 %reduce-scatter.3.cloned.1.call-start = ((), (), s32[]{:S(2)}) async-start(), calls=%async_computation.6 | async-start | bytes 8257536 | tf_op jit(solution)/shard_map/reduce_scatter | solution.py:186
  287.0 9.7 %copy-start.11 = (bf16[256,2560]{1,0:T(8,128)(2,1)S(1)}, bf16[256,2560]{1,0:T(8,128)(2,1)}, u32[]{:S(2)}) copy-start(bf16[256,2560]{1,0:T(8,128)(2,1)} %all-gather.10.cloned.1.call-done) | copy-start | bytes 3932164
  306.9 96.3 %all-gather.12.cloned.1.call-start = ((), (), s32[]{:S(2)}) async-start(), calls=%async_computation.7 | async-start | bytes 2064384 | tf_op jit(solution)/shard_map/all_gather | solution.py:188
  378.1 73.7 %reduce-scatter.5.cloned.1.call-start = ((), (), s32[]{:S(2)}) async-start(), calls=%async_computation.8 | async-start | bytes 2949120 | tf_op jit(solution)/shard_map/reduce_scatter | solution.py:189
  403.3 50.2 %copy-start.1 = (bf16[2048,640]{1,0:T(8,128)(2,1)S(1)}, bf16[2048,640]{1,0:T(8,128)(2,1)}, u32[]{:S(2)}) copy-start(bf16[2048,640]{1,0:T(8,128)(2,1)} %param.41) | copy-start | bytes 7864324
Sparse Core Ops, SparseCore 0:
  15.9 24.7 all-gather.7
  89.2 103.0 all-gather.13
  211.7 29.8 all-reduce.1
  265.6 21.3 all-gather.9
  307.1 67.9 reduce-scatter.2
  378.2 24.9 all-gather.11
  414.3 37.5 reduce-scatter.4
